TPU v7x, 32 devices: a whole 2x2x4 slice. The times are simulated.
32 devices in a mesh: fsdp: 16 (over z, y, x), tp: 2 (over core).
Axes of the slice: x: 2, y: 2, z: 4, core: 2. Of those that a mesh axis runs over, the one named last changes fastest.
Arguments:
- tokens: bfloat16 [12608, 768], P(('fsdp', 'tp')), may hold values from -6 to 6
- cotangent: bfloat16 [12608, 768], P(('fsdp', 'tp')), may hold values from -6 to 6
- image_counts: int32 [16], P('fsdp'), may hold values from 1 to 4, as said below
- w_qkv: bfloat16 [3, 768, 768], P(None, 'fsdp', 'tp'), may hold values from -0.21875 to 0.21875
- b_query: float32 [768], P('tp'), may hold values from -3 to 3
- b_value: float32 [768], P('tp'), may hold values from -3 to 3
- w_out: bfloat16 [768, 768], P('tp', 'fsdp'), may hold values from -0.75 to 0.75
- b_out: float32 [768], replicated, may hold values from -3 to 3
- w_up: bfloat16 [768, 3072], P('fsdp', 'tp'), may hold values from -0.21875 to 0.21875
- b_up: float32 [3072], P('tp'), may hold values from -3 to 3
- w_down: bfloat16 [3072, 768], P('tp', 'fsdp'), may hold values from -0.15625 to 0.15625
- b_down: float32 [768], replicated, may hold values from -3 to 3
- gain_one: float32 [768], replicated, may hold values from 0.1 to 1.9
- shift_one: float32 [768], replicated, may hold values from -3 to 3
- gain_two: float32 [768], replicated, may hold values from 0.1 to 1.9
- shift_two: float32 [768], replicated, may hold values from -3 to 3
Outputs:
- block_out: bfloat16 [12608, 768], P(('fsdp', 'tp'))
- grad_tokens: float32 [12608, 768], P(('fsdp', 'tp'))
- grad_qkv: float32 [3, 768, 768], P(None, 'fsdp', 'tp')
- grad_out: float32 [768, 768], P('tp', 'fsdp')
- grad_up: float32 [768, 3072], P('fsdp', 'tp')
- grad_down: float32 [3072, 768], P('tp', 'fsdp')
- grad_b_query: float32 [768], P('tp')
- grad_b_value: float32 [768], P('tp')
- grad_b_out: float32 [768], replicated
- grad_b_up: float32 [3072], P('tp')
- grad_b_down: float32 [768], replicated
- grad_gain_one: float32 [768], replicated
- grad_shift_one: float32 [768], replicated
- grad_gain_two: float32 [768], replicated
- grad_shift_two: float32 [768], replicated
Inputs may be any that keep to these rules, and one draw needn't show every extreme that they name: `image_counts`: entry f counts the live images among the 4 slots of index f of fsdp; live images come first; entry 0 equals 4.
All inputs are finite; a program needn't handle non-finite values.
Results may differ from a plain program's by a relative error of at most 0.015.
Values may be sent and summed in bfloat16 or wider, within the bound.
A program may use at most 128 MiB of HBM per device.

v0:
```python
import jax
import jax.numpy as jnp
from jax import lax
from jax.sharding import PartitionSpec as P

HEAD_DIM = 64
SEQ = 197
EPS = 1e-06
INV_ROOT_TWO = 0.7071067811865476
INV_ROOT_TWO_PI = 0.3989422804014327


def layer_norm(values, gain, shift):
    center = values - jnp.mean(values, axis=-1, keepdims=True)
    scale_inv = lax.rsqrt(jnp.mean(center * center, axis=-1, keepdims=True) + EPS)
    normal = center * scale_inv
    return (normal, scale_inv, normal * gain + shift)


def norm_back(incoming, normal, scale_inv, gain):
    scaled = incoming * gain
    return scale_inv * (
        scaled
        - jnp.mean(scaled, axis=-1, keepdims=True)
        - normal * jnp.mean(scaled * normal, axis=-1, keepdims=True)
    )


def gelu_parts(pre):
    cdf = 0.5 * (1.0 + lax.erf(pre * INV_ROOT_TWO))
    dens = jnp.exp(-0.5 * pre * pre) * INV_ROOT_TWO_PI
    return (pre * cdf, cdf + pre * dens)


def dotf(left, right):
    return jnp.dot(left, right, preferred_element_type=jnp.float32)


def score_of(query, key):
    return jnp.einsum(
        "bqhe,bkhe->bhqk", query, key, preferred_element_type=jnp.float32
    ) * HEAD_DIM ** (-0.5)


def attend(query, key, value):
    scores = score_of(query, key)
    peak = jnp.max(scores, axis=-1, keepdims=True)
    lse = peak + jnp.log(jnp.sum(jnp.exp(scores - peak), axis=-1, keepdims=True))
    probs = jnp.exp(scores - lse).astype(jnp.bfloat16)
    attended = jnp.einsum("bhqk,bkhe->bqhe", probs, value, preferred_element_type=jnp.float32)
    return (attended.astype(jnp.bfloat16), lse)


def attend_back(query, key, value, lse, attended, dattended):
    scale = HEAD_DIM ** (-0.5)
    delta = jnp.sum(dattended.astype(jnp.float32) * attended.astype(jnp.float32), axis=-1)
    delta = jnp.transpose(delta, (0, 2, 1))[..., None]
    probs_f = jnp.exp(score_of(query, key) - lse)
    probs = probs_f.astype(jnp.bfloat16)
    dvalue = jnp.einsum("bhqk,bqhe->bkhe", probs, dattended, preferred_element_type=jnp.float32)
    dprobs = jnp.einsum("bqhe,bkhe->bhqk", dattended, value, preferred_element_type=jnp.float32)
    dscores = (probs_f * (dprobs - delta)).astype(jnp.bfloat16)
    dquery = jnp.einsum("bhqk,bkhe->bqhe", dscores, key, preferred_element_type=jnp.float32) * scale
    dkey = jnp.einsum("bhqk,bqhe->bkhe", dscores, query, preferred_element_type=jnp.float32) * scale
    return (dquery, dkey, dvalue)


def spread_slice(vector, full_width, offset):
    return lax.dynamic_update_slice_in_dim(jnp.zeros((full_width,), jnp.float32), vector, offset, 0)


def local(
    tokens,
    cotangent,
    image_counts,
    w_qkv,
    b_query,
    b_value,
    w_out,
    b_out,
    w_up,
    b_up,
    w_down,
    b_down,
    gain_one,
    shift_one,
    gain_two,
    shift_two,
):
    rows = tokens.shape[0]
    width = tokens.shape[1]
    slot = lax.axis_index("tp")
    line = (slot * rows + jnp.arange(rows, dtype=jnp.int32)) // SEQ
    live = (line < image_counts[0]).astype(jnp.float32)[:, None]
    xf = tokens.astype(jnp.float32)
    xh1, rs1, n1 = layer_norm(xf, gain_one, shift_one)
    h1g = lax.all_gather(n1.astype(jnp.bfloat16), "tp", axis=0, tiled=True)
    wq_all, wo_all, wu_all, wd_all = (
        lax.all_gather(w_qkv, "fsdp", axis=1, tiled=True),
        lax.all_gather(w_out, "fsdp", axis=1, tiled=True),
        lax.all_gather(w_up, "fsdp", axis=0, tiled=True),
        lax.all_gather(w_down, "fsdp", axis=1, tiled=True),
    )
    group_rows = h1g.shape[0]
    images = group_rows // SEQ
    head_width = wq_all.shape[2]
    hidden_width = wu_all.shape[1]
    shape4 = (images, SEQ, head_width // HEAD_DIM, HEAD_DIM)
    query = (dotf(h1g, wq_all[0]) + b_query).astype(jnp.bfloat16)
    key = dotf(h1g, wq_all[1]).astype(jnp.bfloat16)
    value = (dotf(h1g, wq_all[2]) + b_value).astype(jnp.bfloat16)
    q4, k4, v4 = (query.reshape(shape4), key.reshape(shape4), value.reshape(shape4))
    att4, lse = attend(q4, k4, v4)
    attended = att4.reshape(group_rows, head_width)
    mid = (
        xf
        + lax.psum_scatter(
            dotf(attended, wo_all).astype(jnp.bfloat16), "tp", scatter_dimension=0, tiled=True
        ).astype(jnp.float32)
        + b_out
    )
    xh2, rs2, n2 = layer_norm(mid, gain_two, shift_two)
    h2g = lax.all_gather(n2.astype(jnp.bfloat16), "tp", axis=0, tiled=True)
    pre = dotf(h2g, wu_all) + b_up
    gel, slope = gelu_parts(pre)
    act = gel.astype(jnp.bfloat16)
    block_out = (
        (
            mid
            + lax.psum_scatter(
                dotf(act, wd_all).astype(jnp.bfloat16), "tp", scatter_dimension=0, tiled=True
            ).astype(jnp.float32)
            + b_down
        )
        * live
    ).astype(jnp.bfloat16)
    dout = (cotangent.astype(jnp.float32) * live).astype(jnp.bfloat16)
    doutf = dout.astype(jnp.float32)
    dout_g = lax.all_gather(dout, "tp", axis=0, tiled=True)
    g_down = dotf(act.T, dout_g)
    dpre = dotf(dout_g, wd_all.T) * slope
    g_bup = jnp.sum(dpre, axis=0)
    dpre_b = dpre.astype(jnp.bfloat16)
    g_up = dotf(h2g.T, dpre_b)
    dn2 = lax.psum_scatter(
        dotf(dpre_b, wu_all.T).astype(jnp.bfloat16), "tp", scatter_dimension=0, tiled=True
    ).astype(jnp.float32)
    dmid = doutf + norm_back(dn2, xh2, rs2, gain_two)
    dmid_g = lax.all_gather(dmid.astype(jnp.bfloat16), "tp", axis=0, tiled=True)
    g_out = dotf(attended.T, dmid_g)
    datt = dotf(dmid_g, wo_all.T).astype(jnp.bfloat16)
    dq4, dk4, dv4 = attend_back(q4, k4, v4, lse, att4, datt.reshape(shape4))
    dquery = dq4.reshape(group_rows, head_width)
    dkey = dk4.reshape(group_rows, head_width)
    dvalue = dv4.reshape(group_rows, head_width)
    g_bq = jnp.sum(dquery, axis=0)
    g_bv = jnp.sum(dvalue, axis=0)
    dq_b, dk_b, dv_b = (
        dquery.astype(jnp.bfloat16),
        dkey.astype(jnp.bfloat16),
        dvalue.astype(jnp.bfloat16),
    )
    g_qkv = jnp.stack([dotf(h1g.T, dq_b), dotf(h1g.T, dk_b), dotf(h1g.T, dv_b)])
    dn1_part = dotf(dq_b, wq_all[0].T) + dotf(dk_b, wq_all[1].T) + dotf(dv_b, wq_all[2].T)
    dn1 = lax.psum_scatter(
        dn1_part.astype(jnp.bfloat16), "tp", scatter_dimension=0, tiled=True
    ).astype(jnp.float32)
    grad_tokens = dmid + norm_back(dn1, xh1, rs1, gain_one)
    s_qkv, s_out, s_up, s_down = (
        lax.psum_scatter(g_qkv, "fsdp", scatter_dimension=1, tiled=True),
        lax.psum_scatter(g_out, "fsdp", scatter_dimension=1, tiled=True),
        lax.psum_scatter(g_up, "fsdp", scatter_dimension=0, tiled=True),
        lax.psum_scatter(g_down, "fsdp", scatter_dimension=1, tiled=True),
    )
    head_start = slot * head_width
    hidden_start = slot * hidden_width
    sums = lax.psum(
        (
            spread_slice(g_bq, width, head_start),
            spread_slice(g_bv, width, head_start),
            jnp.sum(dmid, axis=0),
            spread_slice(g_bup, hidden_width * lax.axis_size("tp"), hidden_start),
            jnp.sum(doutf, axis=0),
            jnp.sum(dn1 * xh1, axis=0),
            jnp.sum(dn1, axis=0),
            jnp.sum(dn2 * xh2, axis=0),
            jnp.sum(dn2, axis=0),
        ),
        ("fsdp", "tp"),
    )
    (
        full_bq,
        full_bv,
        sum_bout,
        full_bup,
        sum_bdown,
        sum_gain1,
        sum_shift1,
        sum_gain2,
        sum_shift2,
    ) = sums
    part_bq = lax.dynamic_slice_in_dim(full_bq, head_start, head_width, 0)
    part_bv = lax.dynamic_slice_in_dim(full_bv, head_start, head_width, 0)
    part_bup = lax.dynamic_slice_in_dim(full_bup, hidden_start, hidden_width, 0)
    return (
        block_out,
        grad_tokens,
        s_qkv,
        s_out,
        s_up,
        s_down,
        part_bq,
        part_bv,
        sum_bout,
        part_bup,
        sum_bdown,
        sum_gain1,
        sum_shift1,
        sum_gain2,
        sum_shift2,
    )


def solution(mesh):
    return jax.shard_map(
        local,
        mesh=mesh,
        in_specs=(
            P(("fsdp", "tp"), None),
            P(("fsdp", "tp"), None),
            P("fsdp"),
            P(None, "fsdp", "tp"),
            P("tp"),
            P("tp"),
            P("tp", "fsdp"),
            P(),
            P("fsdp", "tp"),
            P("tp"),
            P("tp", "fsdp"),
            P(),
            P(),
            P(),
            P(),
            P(),
        ),
        out_specs=(
            P(("fsdp", "tp"), None),
            P(("fsdp", "tp"), None),
            P(None, "fsdp", "tp"),
            P("tp", "fsdp"),
            P("fsdp", "tp"),
            P("tp", "fsdp"),
            P("tp"),
            P("tp"),
            P(),
            P("tp"),
            P(),
            P(),
            P(),
            P(),
            P(),
        ),
        check_vma=False,
    )
```

profile of v0, /device:TPU:0, one launch (start us, length us, event | category | flops | bytes accessed | tf_op | source)
XLA Modules:
  0.0 862.7 jit_solution(6002927517635013489)
XLA Ops:
  14.4 45.9 %all_gather.26 = bf16[384,768]{0,1:T(8,128)(2,1)S(1)} all-gather(bf16[384,48]{0,1:T(8,128)(2,1)S(1)} %copy-done.34), channel_id=1, replica_groups=mesh['fsdp'=16,'tp'=2] {'fsdp'}, dimensions={1}, use_global_device_ids=true | all-gather | bytes 626688 | tf_op jit(solution)/shard_map/all_gather | solution.py:100
  62.1 24.3 %all-gather.12.cloned.1.call-done = bf16[3,768,384]{2,1,0:T(8,128)(2,1)} async-done(((bf16[3,48,384]{2,1,0:T(8,128)(2,1)}), bf16[3,768,384]{2,1,0:T(8,128)(2,1)}) %all-gather.12.cloned.1.call-update) | async-done | bytes 1769488 | tf_op jit(solution)/shard_map/all_gather | solution.py:99
  92.2 3.0 convolution_convert_fusion.5
  95.2 3.0 reshape.148
  109.2 3.8 fusion.22
  115.9 4.2 fusion
  123.9 3.1 concatenate
  130.5 2.6 reshape.139
  133.1 4.4 all-gather.20.cloned.1.call-done
  139.0 64.6 %all-gather.14.cloned.1.call-done = bf16[768,1536]{1,0:T(8,128)(2,1)} async-done(((bf16[48,1536]{1,0:T(8,128)(2,1)}), bf16[768,1536]{1,0:T(8,128)(2,1)}) %all-gather.14.cloned.1.call-update) | async-done | bytes 2359312 | tf_op jit(solution)/shard_map/all_gather | solution.py:101
  203.6 6.3 multiply_convert_fusion.1
  209.9 57.5 %all-gather.16.cloned.1.call-done = bf16[1536,768]{0,1:T(8,128)(2,1)} async-done(((bf16[1536,48]{0,1:T(8,128)(2,1)}), bf16[1536,768]{0,1:T(8,128)(2,1)}) %all-gather.16.cloned.1.call-update) | async-done | bytes 2359312 | tf_op jit(solution)/shard_map/all_gather | solution.py:102
  267.4 5.9 fusion.56
  276.8 4.0 fusion.2
  288.4 8.2 all-gather.24.cloned.1.call-done
  299.2 3.0 convolution_convert_fusion.4
  308.7 4.6 bitcast_convert_fusion
  314.7 2.7 convert_element_type.150
  319.0 3.8 multiply_convert_fusion
  325.9 2.7 convert_element_type.148
  328.6 3.5 bitcast_convert_fusion.1
  341.2 6.9 fusion.37
  348.2 6.9 fusion.58
  355.4 5.7 convolution_convert_fusion.1
  365.2 6.8 fusion.54
  378.7 3.1 concatenate.3
  382.7 42.6 %all-reduce.8 = (f32[768]{0:T(1024)S(1)}, f32[768]{0:T(1024)S(1)}, f32[768]{0:T(1024)}, f32[3072]{0:T(1024)S(1)}, f32[768]{0:T(1024)}, /*index=5*/f32[768]{0:T(1...) all-reduce(f32[768]{0:T(1024)S(1)} %dynamic_update_slice.9, ...), channel_id=1, replica_groups=mesh['fsdp'=16,'tp'=2] {'fsdp','tp'}, use_global_device_ids=true, to_apply=%region_20.21 | all-reduce | flops 9216 | bytes 73728 | tf_op jit(solution)/shard_map/psum | solution.py:177
  427.2 4.9 concatenate.1
  432.1 3.5 fusion.28
  435.6 135.8 %reduce-scatter.13.cloned.1.call-done = f32[3,48,384]{2,1,0:T(8,128)} async-done(((f32[3,768,384]{2,1,0:T(8,128)}), f32[3,48,384]{2,1,0:T(8,128)}) %reduce-scatter.13.cloned.1.call-update) | async-done | bytes 221200 | tf_op jit(solution)/shard_map/reduce_scatter | solution.py:170
  571.4 141.7 %reduce-scatter.17.cloned.1.call-done = f32[48,1536]{1,0:T(8,128)} async-done(((f32[768,1536]{1,0:T(8,128)}), f32[48,1536]{1,0:T(8,128)}) %reduce-scatter.17.cloned.1.call-update) | async-done | bytes 294928 | tf_op jit(solution)/shard_map/reduce_scatter | solution.py:172
  713.1 142.6 %reduce-scatter.19.cloned.1.call-done = f32[1536,48]{0,1:T(8,128)} async-done(((f32[1536,768]{0,1:T(8,128)}), f32[1536,48]{0,1:T(8,128)}) %reduce-scatter.19.cloned.1.call-update) | async-done | bytes 294928 | tf_op jit(solution)/shard_map/reduce_scatter | solution.py:173
  (192 shorter events, 84.9 us)
Async XLA Ops:
  7.2 53.1 %all-gather.18.cloned.1.call-start = ((), (), s32[]{:S(2)}) async-start(), calls=%async_computation.11 | async-start | bytes 1843200 | tf_op jit(solution)/shard_map/all_gather | solution.py:97
  8.6 4.1 copy-start.20
  11.2 75.2 %all-gather.12.cloned.1.call-start = ((), (), s32[]{:S(2)}) async-start(), calls=%async_computation.4 | async-start | bytes 1880064 | tf_op jit(solution)/shard_map/all_gather | solution.py:99
  12.0 118.5 %all-gather.22.cloned.1.call-start = ((), (), s32[]{:S(2)}) async-start(), calls=%async_computation.13 | async-start | bytes 1843200 | tf_op jit(solution)/shard_map/all_gather | solution.py:139
  14.3 123.1 %all-gather.20.cloned.1.call-start = ((), (), s32[]{:S(2)}) async-start(), calls=%async_computation.12 | async-start | bytes 1843200 | tf_op jit(solution)/shard_map/all_gather | solution.py:123
  60.3 54.7 %copy-start.23 = (bf16[384,768]{0,1:T(8,128)(2,1)}, bf16[384,768]{0,1:T(8,128)(2,1)S(1)}, u32[]{:S(2)}) copy-start(bf16[384,768]{0,1:T(8,128)(2,1)S(1)} %all_gather.26) | copy-start | bytes 1769476
  60.3 26.1 %copy-start.42 = (f32[384]{0:T(512)S(1)}, f32[384]{0:T(512)}, u32[]{:S(2)}) copy-start(f32[384]{0:T(512)} %param.20) | copy-start | bytes 4612
  62.1 30.1 %copy-start.26 = (bf16[788,768]{1,0:T(8,128)(2,1)}, bf16[788,768]{1,0:T(8,128)(2,1)S(1)}, u32[]{:S(2)}) copy-start(bf16[788,768]{1,0:T(8,128)(2,1)S(1)} %reshape.135) | copy-start | bytes 3631108
  92.2 7.9 copy-start.8
  115.9 6.7 copy-start.39
  115.9 11.0 %copy-start.31 = (f32[768]{0:T(1024)S(1)}, f32[768]{0:T(1024)}, u32[]{:S(2)}) copy-start(f32[768]{0:T(1024)} %param.23) | copy-start | bytes 9220
  120.1 3.7 collective-permute-start
  129.2 74.3 %all-gather.14.cloned.1.call-start = ((), (), s32[]{:S(2)}) async-start(), calls=%async_computation.5 | async-start | bytes 2506752 | tf_op jit(solution)/shard_map/all_gather | solution.py:101
  129.8 137.5 %all-gather.16.cloned.1.call-start = ((), (), s32[]{:S(2)}) async-start(), calls=%async_computation.6 | async-start | bytes 2506752 | tf_op jit(solution)/shard_map/all_gather | solution.py:102
  130.4 166.3 %all-gather.24.cloned.1.call-start = ((), (), s32[]{:S(2)}) async-start(), calls=%async_computation.14 | async-start | bytes 1843200 | tf_op jit(solution)/shard_map/all_gather | solution.py:149
  133.1 70.5 %copy-start.41 = (f32[1536]{0:T(1024)S(1)}, f32[1536]{0:T(1024)}, u32[]{:S(2)}) copy-start(f32[1536]{0:T(1024)} %param.25) | copy-start | bytes 18436
  139.0 70.9 %copy-start.11 = (bf16[788,768]{1,0:T(8,128)(2,1)}, bf16[788,768]{1,0:T(8,128)(2,1)S(1)}, u32[]{:S(2)}) copy-start(bf16[788,768]{1,0:T(8,128)(2,1)S(1)} %reshape.137) | copy-start | bytes 3631108
  267.4 7.3 copy-start.40
  280.8 3.1 collective-permute-start.2
  288.4 10.9 %copy-start.24 = (bf16[384,768]{0,1:T(8,128)(2,1)S(1)}, bf16[384,768]{0,1:T(8,128)(2,1)}, u32[]{:S(2)}) copy-start(bf16[384,768]{0,1:T(8,128)(2,1)} %copy-done.23) | copy-start | bytes 1769476
  288.4 147.2 %reduce-scatter.15.cloned.1.call-start = ((), (), s32[]{:S(2)}) async-start(), calls=%async_computation.8 | async-start | bytes 1253376 | tf_op jit(solution)/shard_map/reduce_scatter | solution.py:171
  308.4 263.0 %reduce-scatter.13.cloned.1.call-start = ((), (), s32[]{:S(2)}) async-start(), calls=%async_computation.7 | async-start | bytes 3760128 | tf_op jit(solution)/shard_map/reduce_scatter | solution.py:170
  324.3 4.2 copy-start.7
  340.9 372.2 %reduce-scatter.17.cloned.1.call-start = ((), (), s32[]{:S(2)}) async-start(), calls=%async_computation.9 | async-start | bytes 5013504 | tf_op jit(solution)/shard_map/reduce_scatter | solution.py:172
  348.1 507.6 %reduce-scatter.19.cloned.1.call-start = ((), (), s32[]{:S(2)}) async-start(), calls=%async_computation.10 | async-start | bytes 5013504 | tf_op jit(solution)/shard_map/reduce_scatter | solution.py:173
  355.4 5.7 copy-start.25
  372.1 4.9 copy-start.18
  372.1 4.5 copy-start.10
  372.9 5.8 collective-permute-start.3
  376.9 50.3 %collective-permute-start.1 = (bf16[6,768]{1,0:T(8,128)(2,1)S(1)}, bf16[6,768]{1,0:T(8,128)(2,1)S(1)}, u32[]{:S(2)}, u32[]{:S(2)}) collective-permute-start(bf16[6,768]{1,0:T(8,128)(2,1)S(1)} %slice.19), channel_id=1, source_target_pairs={{0,1},{2,3},{4,5},{6,7},{8,9},{10,11},{12,13},{14,15},{16,17},{18,... | collective-permute-start | bytes 27656
  378.7 4.0 copy-start.35
  381.8 50.4 %copy-start.38 = (f32[768]{0:T(1024)S(1)}, f32[768]{0:T(1024)}, u32[]{:S(2)}) copy-start(f32[768]{0:T(1024)} %param.27) | copy-start | bytes 9220
  (27 other events, 56.6 us)
Sparse Core Ops, SparseCore 0:
  11.3 11.9 all-gather.17
  26.0 60.3 all-gather.11
  87.9 8.0 all-gather.21
  129.4 8.0 all-gather.19
  140.1 63.4 all-gather.13
  206.2 61.0 all-gather.15
  288.5 8.1 all-gather.23
  308.6 124.7 reduce-scatter.14
  439.1 132.3 reduce-scatter.12
  577.0 136.0 reduce-scatter.16
  719.7 135.9 reduce-scatter.18
where the time goes:
time: 873 us; the launch traced here: 863 us
  waiting for transfers between devices  582 us (67%)
  blocking collectives  104 us (12%)
  matrix products  72 us (8%)
  local copies, waits for them, and re-layouts  58.7 us (7%)
  other arithmetic  21.3 us (2%)
  between operations  16.4 us (2%)
  starting transfers between devices  9.01 us (1%)
    reduce_scatter x1, waiting for transfers between devices, local(): lax.psum_scatter(g_down, 'fsdp', scatter_dimension=1, tiled=True)  143 us
    reduce_scatter x1, waiting for transfers between devices, local(): lax.psum_scatter(g_up, 'fsdp', scatter_dimension=0, tiled=True)  142 us
    reduce_scatter x1, waiting for transfers between devices, local(): lax.psum_scatter(g_qkv, 'fsdp', scatter_dimension=1, tiled=True)  136 us
    all_gather x1, waiting for transfers between devices, local(): lax.all_gather(w_up, 'fsdp', axis=0, tiled=True)  64.6 us
    all_gather x1, waiting for transfers between devices, local(): lax.all_gather(w_down, 'fsdp', axis=1, tiled=True)  57.5 us
    dot_general x18, matrix products, dotf(): return jnp.dot(left, right, preferred_element_type=jnp.float32)  54.5 us
    all_gather x1, blocking collectives, local(): lax.all_gather(w_out, 'fsdp', axis=1, tiled=True)  45.9 us
    psum x1, blocking collectives, local(): lax.psum((spread_slice(g_bq, width, head_start), spread_slice(g_bv, width...  42.6 us
  transfers between devices with their start and end apart: 15, of which 9 were waited for; matrix products, arithmetic and copies ran while one was open for 15% of the time, Pallas kernels for 0%

commit v1 on v0

--- a/solution.py
+++ b/solution.py
@@ -175,18 +175,21 @@
     head_start = slot * head_width
     hidden_start = slot * hidden_width
     sums = lax.psum(
-        (
-            spread_slice(g_bq, width, head_start),
-            spread_slice(g_bv, width, head_start),
-            jnp.sum(dmid, axis=0),
-            spread_slice(g_bup, hidden_width * lax.axis_size("tp"), hidden_start),
-            jnp.sum(doutf, axis=0),
-            jnp.sum(dn1 * xh1, axis=0),
-            jnp.sum(dn1, axis=0),
-            jnp.sum(dn2 * xh2, axis=0),
-            jnp.sum(dn2, axis=0),
+        lax.psum(
+            (
+                spread_slice(g_bq, width, head_start),
+                spread_slice(g_bv, width, head_start),
+                jnp.sum(dmid, axis=0),
+                spread_slice(g_bup, hidden_width * lax.axis_size("tp"), hidden_start),
+                jnp.sum(doutf, axis=0),
+                jnp.sum(dn1 * xh1, axis=0),
+                jnp.sum(dn1, axis=0),
+                jnp.sum(dn2 * xh2, axis=0),
+                jnp.sum(dn2, axis=0),
+            ),
+            "tp",
         ),
-        ("fsdp", "tp"),
+        "fsdp",
     )
     (
         full_bq,

time: 873 us -> 868 us (level)
  blocking collectives: 104 us -> 147 us
  waiting for transfers between devices: 582 us -> 540 us
    psum x0 -> x1, blocking collectives: none -> 78.3 us  [local(): lax.psum(lax.psum((spread_slice(g_bq, width, head_start), spread_slice(g_...]
    reduce_scatter x1, waiting for transfers between devices: 136 us -> 96.6 us  [local(): lax.psum_scatter(g_qkv, 'fsdp', scatter_dimension=1, tiled=True)]
    psum x1, blocking collectives: 42.6 us -> 3.55 us  [local(): lax.psum((spread_slice(g_bq, width, head_start), spread_slice(g_bv, width...]
    unnamed x101 -> x97, local copies, waits for them, and re-layouts: 27.2 us -> 25.4 us
  transfers between devices with their start and end apart: 15 -> 15, of which waited for: 9 -> 9; matrix products, arithmetic and copies ran while one was open for 15% -> 14% of each run, Pallas kernels for 0% -> 0%
where the time goes in v1:
time: 868 us; the launch traced here: 858 us
  waiting for transfers between devices  540 us (62%)
  blocking collectives  147 us (17%)
  matrix products  72.4 us (8%)
  local copies, waits for them, and re-layouts  52.9 us (6%)
  other arithmetic  20.7 us (2%)
  between operations  16.3 us (2%)
  starting transfers between devices  8.83 us (1%)
    reduce_scatter x1, waiting for transfers between devices, local(): lax.psum_scatter(g_down, 'fsdp', scatter_dimension=1, tiled=True)  143 us
    reduce_scatter x1, waiting for transfers between devices, local(): lax.psum_scatter(g_up, 'fsdp', scatter_dimension=0, tiled=True)  142 us
    reduce_scatter x1, waiting for transfers between devices, local(): lax.psum_scatter(g_qkv, 'fsdp', scatter_dimension=1, tiled=True)  96.6 us
    psum x1, blocking collectives, local(): lax.psum(lax.psum((spread_slice(g_bq, width, head_start), spread_slice(g_...  78.3 us
    all_gather x1, waiting for transfers between devices, local(): lax.all_gather(w_up, 'fsdp', axis=0, tiled=True)  64.6 us
    all_gather x1, waiting for transfers between devices, local(): lax.all_gather(w_down, 'fsdp', axis=1, tiled=True)  57.5 us
    dot_general x18, matrix products, dotf(): return jnp.dot(left, right, preferred_element_type=jnp.float32)  55 us
    all_gather x1, blocking collectives, local(): lax.all_gather(w_out, 'fsdp', axis=1, tiled=True)  49.5 us
  transfers between devices with their start and end apart: 15, of which 9 were waited for; matrix products, arithmetic and copies ran while one was open for 14% of the time, Pallas kernels for 0%

profile of v1, /device:TPU:0, one launch (start us, length us, event | category | flops | bytes accessed | tf_op | source)
XLA Modules:
  0.0 858.0 jit_solution(12154536813779960841)
XLA Ops:
  13.8 49.5 %all_gather.26 = bf16[384,768]{0,1:T(8,128)(2,1)} all-gather(bf16[384,48]{0,1:T(8,128)(2,1)S(1)} %copy-done.33), channel_id=1, replica_groups=mesh['fsdp'=16,'tp'=2] {'fsdp'}, dimensions={1}, use_global_device_ids=true | all-gather | bytes 626688 | tf_op jit(solution)/shard_map/all_gather | solution.py:100
  64.9 21.6 %all-gather.12.cloned.1.call-done = bf16[3,768,384]{2,1,0:T(8,128)(2,1)} async-done(((bf16[3,48,384]{2,1,0:T(8,128)(2,1)}), bf16[3,768,384]{2,1,0:T(8,128)(2,1)}) %all-gather.12.cloned.1.call-update) | async-done | bytes 1769488 | tf_op jit(solution)/shard_map/all_gather | solution.py:99
  86.4 2.7 fusion.21
  92.3 2.6 convolution_convert_fusion.5
  105.7 3.8 fusion.22
  112.5 4.3 fusion
  125.3 2.6 reshape.139
  127.9 4.3 all-gather.20.cloned.1.call-done
  133.8 64.6 %all-gather.14.cloned.1.call-done = bf16[768,1536]{1,0:T(8,128)(2,1)} async-done(((bf16[48,1536]{1,0:T(8,128)(2,1)}), bf16[768,1536]{1,0:T(8,128)(2,1)}) %all-gather.14.cloned.1.call-update) | async-done | bytes 2359312 | tf_op jit(solution)/shard_map/all_gather | solution.py:101
  198.4 6.3 multiply_convert_fusion.1
  204.6 57.5 %all-gather.16.cloned.1.call-done = bf16[1536,768]{0,1:T(8,128)(2,1)} async-done(((bf16[1536,48]{0,1:T(8,128)(2,1)}), bf16[1536,768]{0,1:T(8,128)(2,1)}) %all-gather.16.cloned.1.call-update) | async-done | bytes 2359312 | tf_op jit(solution)/shard_map/all_gather | solution.py:102
  262.2 5.9 fusion.56
  271.6 4.0 fusion.2
  283.2 8.2 all-gather.24.cloned.1.call-done
  294.0 3.0 convolution_convert_fusion.4
  303.5 4.6 bitcast_convert_fusion
  309.6 2.7 convert_element_type.150
  313.9 3.8 multiply_convert_fusion
  320.7 2.7 convert_element_type.148
  323.4 3.5 bitcast_convert_fusion.1
  336.0 6.9 fusion.37
  343.0 6.9 fusion.58
  350.2 5.7 convolution_convert_fusion.1
  360.0 6.8 fusion.54
  373.5 3.1 concatenate.3
  377.4 3.5 all-reduce.9
  381.0 78.3 %all-reduce.8 = (f32[768]{0:T(1024)S(1)}, f32[768]{0:T(1024)S(1)}, f32[768]{0:T(1024)}, f32[3072]{0:T(1024)S(1)}, f32[768]{0:T(1024)}, /*index=5*/f32[768]{0:T(1...) all-reduce(f32[768]{0:T(1024)S(1)} %get-tuple-element.32, ...), channel_id=1, replica_groups=mesh['fsdp'=16,'tp'=2] {'fsdp'}, use_global_device_ids=true, to_apply=%region_21.22 | all-reduce | flops 9216 | bytes 73728 | tf_op jit(solution)/shard_map/psum | solution.py:177
  461.3 5.0 concatenate.1
  466.3 3.4 fusion.28
  469.7 96.6 %reduce-scatter.13.cloned.1.call-done = f32[3,48,384]{2,1,0:T(8,128)} async-done(((f32[3,768,384]{2,1,0:T(8,128)}), f32[3,48,384]{2,1,0:T(8,128)}) %reduce-scatter.13.cloned.1.call-update) | async-done | bytes 221200 | tf_op jit(solution)/shard_map/reduce_scatter | solution.py:170
  566.3 141.9 %reduce-scatter.17.cloned.1.call-done = f32[48,1536]{1,0:T(8,128)} async-done(((f32[768,1536]{1,0:T(8,128)}), f32[48,1536]{1,0:T(8,128)}) %reduce-scatter.17.cloned.1.call-update) | async-done | bytes 294928 | tf_op jit(solution)/shard_map/reduce_scatter | solution.py:172
  708.3 142.8 %reduce-scatter.19.cloned.1.call-done = f32[1536,48]{0,1:T(8,128)} async-done(((f32[1536,768]{0,1:T(8,128)}), f32[1536,48]{0,1:T(8,128)}) %reduce-scatter.19.cloned.1.call-update) | async-done | bytes 294928 | tf_op jit(solution)/shard_map/reduce_scatter | solution.py:173
  (189 shorter events, 82.6 us)
Async XLA Ops:
  7.2 56.1 %all-gather.18.cloned.1.call-start = ((), (), s32[]{:S(2)}) async-start(), calls=%async_computation.11 | async-start | bytes 1843200 | tf_op jit(solution)/shard_map/all_gather | solution.py:97
  8.6 4.1 copy-start.19
  11.2 75.2 %all-gather.12.cloned.1.call-start = ((), (), s32[]{:S(2)}) async-start(), calls=%async_computation.4 | async-start | bytes 1880064 | tf_op jit(solution)/shard_map/all_gather | solution.py:99
  12.0 113.4 %all-gather.22.cloned.1.call-start = ((), (), s32[]{:S(2)}) async-start(), calls=%async_computation.13 | async-start | bytes 1843200 | tf_op jit(solution)/shard_map/all_gather | solution.py:139
  13.8 118.5 %all-gather.20.cloned.1.call-start = ((), (), s32[]{:S(2)}) async-start(), calls=%async_computation.12 | async-start | bytes 1843200 | tf_op jit(solution)/shard_map/all_gather | solution.py:123
  63.3 23.1 %copy-start.40 = (f32[384]{0:T(512)S(1)}, f32[384]{0:T(512)}, u32[]{:S(2)}) copy-start(f32[384]{0:T(512)} %param.20) | copy-start | bytes 4612
  64.9 21.6 %copy-start.25 = (bf16[788,768]{1,0:T(8,128)(2,1)}, bf16[788,768]{1,0:T(8,128)(2,1)S(1)}, u32[]{:S(2)}) copy-start(bf16[788,768]{1,0:T(8,128)(2,1)S(1)} %reshape.135) | copy-start | bytes 3631108
  92.3 6.6 copy-start.8
  105.7 3.8 copy-start.3
  112.5 6.6 copy-start.37
  112.5 9.3 %copy-start.30 = (f32[768]{0:T(1024)S(1)}, f32[768]{0:T(1024)}, u32[]{:S(2)}) copy-start(f32[768]{0:T(1024)} %param.23) | copy-start | bytes 9220
  116.8 3.5 collective-permute-start
  124.1 74.3 %all-gather.14.cloned.1.call-start = ((), (), s32[]{:S(2)}) async-start(), calls=%async_computation.5 | async-start | bytes 2506752 | tf_op jit(solution)/shard_map/all_gather | solution.py:101
  124.7 137.5 %all-gather.16.cloned.1.call-start = ((), (), s32[]{:S(2)}) async-start(), calls=%async_computation.6 | async-start | bytes 2506752 | tf_op jit(solution)/shard_map/all_gather | solution.py:102
  125.3 166.2 %all-gather.24.cloned.1.call-start = ((), (), s32[]{:S(2)}) async-start(), calls=%async_computation.14 | async-start | bytes 1843200 | tf_op jit(solution)/shard_map/all_gather | solution.py:149
  127.9 70.4 %copy-start.39 = (f32[1536]{0:T(1024)S(1)}, f32[1536]{0:T(1024)}, u32[]{:S(2)}) copy-start(f32[1536]{0:T(1024)} %param.25) | copy-start | bytes 18436
  133.8 70.9 %copy-start.11 = (bf16[788,768]{1,0:T(8,128)(2,1)}, bf16[788,768]{1,0:T(8,128)(2,1)S(1)}, u32[]{:S(2)}) copy-start(bf16[788,768]{1,0:T(8,128)(2,1)S(1)} %reshape.137) | copy-start | bytes 3631108
  262.2 7.3 copy-start.38
  275.7 3.1 collective-permute-start.2
  283.2 10.9 %copy-start.23 = (bf16[384,768]{0,1:T(8,128)(2,1)S(1)}, bf16[384,768]{0,1:T(8,128)(2,1)}, u32[]{:S(2)}) copy-start(bf16[384,768]{0,1:T(8,128)(2,1)} %all_gather.26) | copy-start | bytes 1769476
  283.2 186.6 %reduce-scatter.15.cloned.1.call-start = ((), (), s32[]{:S(2)}) async-start(), calls=%async_computation.8 | async-start | bytes 1253376 | tf_op jit(solution)/shard_map/reduce_scatter | solution.py:171
  303.3 263.0 %reduce-scatter.13.cloned.1.call-start = ((), (), s32[]{:S(2)}) async-start(), calls=%async_computation.7 | async-start | bytes 3760128 | tf_op jit(solution)/shard_map/reduce_scatter | solution.py:170
  313.9 3.9 copy-start.9
  319.2 4.2 copy-start.7
  335.7 372.5 %reduce-scatter.17.cloned.1.call-start = ((), (), s32[]{:S(2)}) async-start(), calls=%async_computation.9 | async-start | bytes 5013504 | tf_op jit(solution)/shard_map/reduce_scatter | solution.py:172
  342.9 508.1 %reduce-scatter.19.cloned.1.call-start = ((), (), s32[]{:S(2)}) async-start(), calls=%async_computation.10 | async-start | bytes 5013504 | tf_op jit(solution)/shard_map/reduce_scatter | solution.py:173
  350.2 5.7 copy-start.24
  366.9 4.9 copy-start.18
  366.9 4.5 copy-start.10
  367.7 5.8 collective-permute-start.3
  371.7 89.6 %collective-permute-start.1 = (bf16[6,768]{1,0:T(8,128)(2,1)S(1)}, bf16[6,768]{1,0:T(8,128)(2,1)S(1)}, u32[]{:S(2)}, u32[]{:S(2)}) collective-permute-start(bf16[6,768]{1,0:T(8,128)(2,1)S(1)} %slice.19), channel_id=1, source_target_pairs={{0,1},{2,3},{4,5},{6,7},{8,9},{10,11},{12,13},{14,15},{16,17},{18,... | collective-permute-start | bytes 27656
  376.6 89.7 %copy-start.36 = (f32[768]{0:T(1024)S(1)}, f32[768]{0:T(1024)}, u32[]{:S(2)}) copy-start(f32[768]{0:T(1024)} %param.27) | copy-start | bytes 9220
  (25 other events, 45.9 us)
Sparse Core Ops, SparseCore 0:
  11.3 11.9 all-gather.17
  26.0 60.3 all-gather.11
  88.0 8.0 all-gather.21
  124.2 7.9 all-gather.19
  134.9 63.4 all-gather.13
  201.0 61.0 all-gather.15
  283.3 8.1 all-gather.23
  303.4 124.8 reduce-scatter.14
  434.0 132.2 reduce-scatter.12
  571.9 136.3 reduce-scatter.16
  714.8 136.1 reduce-scatter.18
